TPU v7x, 128 devices: a whole 4x4x4 slice. The times are simulated.
128 devices in a mesh: iy: 4 (over z), ix: 2 (over core), gz: 16 (over x, y).
Axes of the slice: x: 4, y: 4, z: 4, core: 2. Of those that a mesh axis runs over, the one named last changes fastest.
Arguments:
- fields: float32 [2, 512, 512, 512], P(None, 'gz', 'iy', 'ix'), may hold values from -6 to 6
- palette: float32 [2, 3], replicated, may hold values from -2 to 2
Outputs:
- image: float32 [4, 512, 512], P(None, ('iy', 'gz'), 'ix')
All inputs are finite; a program needn't handle non-finite values.
Results may differ from a plain program's by a relative error of at most 0.0003.
Values sent between devices are 32-bit elements; how exact they have to be, the bound alone decides.
A program may use at most 128 MiB of HBM per device.

v0:
```python
import jax
import jax.numpy as jnp
from jax import lax
from jax.sharding import PartitionSpec as P


def padded_2(value, sides, width):
    for axis, dim in sides:
        peers, length = (lax.axis_size(axis), value.shape[dim])
        up = [(i, (i + 1) % peers) for i in range(peers - 1)]
        down = [(j, i) for i, j in up]
        last = lax.slice_in_dim(value, length - width, length, axis=dim)
        leading = lax.slice_in_dim(value, 0, width, axis=dim)
        before = lax.ppermute(last, axis, up)
        after = lax.ppermute(leading, axis, down)
        value = jnp.concatenate([before, value, after], axis=dim)
    return value


def carried_in(part, axis, combine, identity):
    place = lax.axis_index(axis)
    gathered = lax.all_gather(part, axis)
    state = jnp.zeros_like(part) + jnp.asarray(identity, part.dtype)

    def one(step, state):
        return combine(state, lax.dynamic_index_in_dim(gathered, step, 0, False))

    return lax.fori_loop(0, place, one, state)


def central(field):
    grad_z = 0.5 * (field[2:, 1:-1, 1:-1] - field[:-2, 1:-1, 1:-1])
    grad_y = 0.5 * (field[1:-1, 2:, 1:-1] - field[1:-1, :-2, 1:-1])
    grad_x = 0.5 * (field[1:-1, 1:-1, 2:] - field[1:-1, 1:-1, :-2])
    return (grad_z, grad_y, grad_x)


def shade(padded, palette):
    density = padded[0]
    heat = padded[1]
    grad_z, grad_y, grad_x = central(density)
    slope = grad_z * grad_z + grad_y * grad_y + grad_x * grad_x
    heat_z, heat_y, heat_x = central(heat)
    edges = heat_z * heat_z + heat_y * heat_y + heat_x * heat_x
    inner = density[1:-1, 1:-1, 1:-1]
    optical = 0.004 * jnp.exp(inner) * (0.25 + slope / (1.0 + slope))
    facing = jnp.abs(0.36 * grad_z + 0.48 * grad_y + 0.8 * grad_x) / jnp.sqrt(1.0 + slope)
    lighting = (0.3 + 0.7 * facing) * (0.5 + edges / (1.0 + edges))
    heat_inner = heat[1:-1, 1:-1, 1:-1]
    emitted = (
        jax.nn.sigmoid(
            palette[0][:, None, None, None] * heat_inner[None] + palette[1][:, None, None, None]
        )
        * lighting[None]
    )
    return (optical, emitted)


def clamp_edges(padded, dim_pos, place, extent):
    length = padded.shape[dim_pos]
    lower = lax.slice_in_dim(padded, 0, 1, axis=dim_pos)
    first_layer = lax.slice_in_dim(padded, 1, 2, axis=dim_pos)
    middle = lax.slice_in_dim(padded, 1, length - 1, axis=dim_pos)
    last_layer = lax.slice_in_dim(padded, length - 2, length - 1, axis=dim_pos)
    upper = lax.slice_in_dim(padded, length - 1, length, axis=dim_pos)
    lower = jnp.where(place == 0, first_layer, lower)
    upper = jnp.where(place == extent - 1, last_layer, upper)
    return jnp.concatenate([lower, middle, upper], axis=dim_pos)


def add_maps(earlier, later):
    return earlier + later


def body(fields, palette):
    padded = padded_2(fields, (("iy", 2), ("ix", 3), ("gz", 1)), 1)
    padded = clamp_edges(padded, 1, lax.axis_index("gz"), lax.axis_size("gz"))
    padded = clamp_edges(padded, 2, lax.axis_index("iy"), lax.axis_size("iy"))
    padded = clamp_edges(padded, 3, lax.axis_index("ix"), lax.axis_size("ix"))
    optical, emitted = shade(padded, palette)
    before = jnp.cumsum(optical, axis=0) - optical
    weight = jnp.exp(-before) * (1.0 - jnp.exp(-optical))
    partial_value = jnp.sum(weight[None] * emitted, axis=1)
    brick_depth = jnp.sum(optical, axis=0)
    in_front = carried_in(brick_depth, "gz", add_maps, jnp.zeros_like(brick_depth))
    weighted = jnp.concatenate(
        [partial_value * jnp.exp(-in_front)[None], brick_depth[None]], axis=0
    )
    summed = lax.psum_scatter(weighted, "gz", scatter_dimension=1, tiled=True)
    colors = summed[:3]
    optical_sum = summed[3]
    return jnp.concatenate([colors, (1.0 - jnp.exp(-optical_sum))[None]], axis=0)


def solution(mesh):
    placed = (P(None, "gz", "iy", "ix"), P())
    return jax.shard_map(
        body, mesh=mesh, in_specs=placed, out_specs=P(None, ("iy", "gz"), "ix"), check_vma=False
    )
```

profile of v0, /device:TPU:1, one launch (start us, length us, event | category | flops | bytes accessed | tf_op | source)
XLA Modules:
  0.0 318.8 jit_solution(7753616506657280350)
XLA Ops:
  6.5 1.3 fusion.21
  7.8 4.4 %collective-permute-start = (f32[2,32,1,256]{3,2,1,0:T(1,128)S(1)}, f32[2,32,1,256]{3,2,1,0:T(1,128)S(1)}, u32[]{:S(2)}, u32[]{:S(2)}) collective-permute-start(f32[2,32,1,256]{3,2,1,0:T(1,128)S(1)} %get-tuple-element.47), channel_id=1, source_target_pairs={{0,32},{32,64},{64,96},{1,33},{33,65},{65,97},{2,34},{34,66},{66,9... | collective-permute-start | bytes 196616 | tf_op jit(solution)/shard_map/ppermute | solution.py:14
  12.2 1.3 collective-permute-start.1
  13.5 3.9 %collective-permute-done.1 = f32[2,32,1,256]{3,2,1,0:T(1,128)S(1)} collective-permute-done((f32[2,32,1,256]{3,2,1,0:T(1,128)S(1)}, f32[2,32,1,256]{3,2,1,0:T(1,128)S(1)}, u32[]{:S(2)}, u32[]{:S(2)}) %collective-permute-start.1) | collective-permute-done | bytes 65568 | tf_op jit(solution)/shard_map/ppermute | solution.py:15
  17.4 4.0 %pad_maximum_fusion.3 = f32[2,32,130,256]{3,2,1,0:T(8,128)S(1)} fusion(f32[2,32,1,256]{3,2,1,0:T(1,128)S(1)} %collective-permute-done.1, f32[2,32,128,256]{3,2,1,0:T(8,128)} %param.4, f32[2,32,1,256]{3,2,1,0:T(1,128)S(1)} %collective-permute-done), kind=kLoop, calls=%fused_computation.5 | loop fusion | flops 4259840 | bytes 17039360 | tf_op jit(solution)/shard_map/concatenate | solution.py:16
  21.4 4.8 %fusion.20 = (f32[2,32,130,1]{3,2,1,0:T(8,128)}, f32[2,32,130,1]{3,2,1,0:T(8,128)}) fusion(f32[2,32,130,256]{3,2,1,0:T(8,128)S(1)} %pad_maximum_fusion.3), kind=kLoop, calls=%fused_computation.57 | loop fusion | bytes 133120 | tf_op jit(solution)/shard_map/slice | solution.py:12
  26.2 4.0 %copy.7 = f32[2,32,130,1]{2,1,3,0:T(8,128)S(1)} copy(f32[2,32,130,1]{3,2,1,0:T(8,128)} %get-tuple-element.45) | data formatting | bytes 66560 | tf_op jit(solution)/shard_map/slice | solution.py:12
  30.2 1.3 collective-permute-start.2
  31.5 4.0 %copy.8 = f32[2,32,130,1]{2,1,3,0:T(8,128)S(1)} copy(f32[2,32,130,1]{3,2,1,0:T(8,128)} %get-tuple-element.46) | data formatting | bytes 66560 | tf_op jit(solution)/shard_map/slice | solution.py:13
  35.6 3.8 %collective-permute-start.3 = (f32[2,32,130,1]{2,1,3,0:T(8,128)S(1)}, f32[2,32,130,1]{2,1,3,0:T(8,128)S(1)}, u32[]{:S(2)}, u32[]{:S(2)}) collective-permute-start(f32[2,32,130,1]{2,1,3,0:T(8,128)S(1)} %copy.8), channel_id=1, source_target_pairs={{16,0},{17,1},{18,2},{19,3},{20,4},{21,5},{22,6},{23,7},{24,8},{25... | collective-permute-start | bytes 99848 | tf_op jit(solution)/shard_map/ppermute | solution.py:15
  39.4 2.9 copy.9
  42.3 2.9 copy.10
  45.2 1.3 pad_maximum_fusion.5
  46.5 3.2 %collective-permute-start.4 = (f32[2,1,130,258]{3,2,1,0:T(8,128)S(1)}, f32[2,1,130,258]{3,2,1,0:T(8,128)S(1)}, u32[]{:S(2)}, u32[]{:S(2)}) collective-permute-start(f32[2,1,130,258]{3,2,1,0:T(8,128)S(1)} %pad_maximum_fusion.5), channel_id=1, source_target_pairs={{0,1},{1,2},{2,3},{3,4},{4,5},{5,6},{6,7},{7,8},{8,9},{9,10},{10,1... | collective-permute-start | bytes 804968 | tf_op jit(solution)/shard_map/ppermute | solution.py:14
  49.8 9.3 %collective-permute-done.4 = f32[2,1,130,258]{3,2,1,0:T(8,128)S(1)} collective-permute-done((f32[2,1,130,258]{3,2,1,0:T(8,128)S(1)}, f32[2,1,130,258]{3,2,1,0:T(8,128)S(1)}, u32[]{:S(2)}, u32[]{:S(2)}) %collective-permute-start.4) | collective-permute-done | bytes 268352 | tf_op jit(solution)/shard_map/ppermute | solution.py:14
  60.4 1.5 collective-permute-start.5
  61.9 12.0 %collective-permute-done.5 = f32[2,1,130,258]{3,2,1,0:T(8,128)S(1)} collective-permute-done((f32[2,1,130,258]{3,2,1,0:T(8,128)S(1)}, f32[2,1,130,258]{3,2,1,0:T(8,128)S(1)}, u32[]{:S(2)}, u32[]{:S(2)}) %collective-permute-start.5) | collective-permute-done | bytes 268352 | tf_op jit(solution)/shard_map/ppermute | solution.py:15
  74.0 15.2 %pad_maximum_fusion = f32[2,34,130,258]{3,2,1,0:T(8,128)} fusion(f32[2,1,130,258]{3,2,1,0:T(8,128)S(1)} %broadcast_select_fusion.1, f32[2,32,130,1]{3,2,1,0:T(8,128)} %copy.10, f32[2,32,1,256]{3,2,1,0:T(1,128)S(1)} %collective-permute-done.1, f32[2,32,128,256]{3,2,1,0:T(8,128)} %param.4, f32[2,32,1,256]{3,2,1,0:T(1,128)S(1)} %collective-permute-done, ...), kind=kLoop, calls=%fused_computation.1 | loop fusion | flops 13684320 | bytes 18245760 | tf_op jit(solution)/shard_map/concatenate | solution.py:68
  89.2 11.9 %slice.148 = f32[2,34,128,258]{3,2,1,0:T(8,128)} slice(f32[2,34,130,258]{3,2,1,0:T(8,128)} %pad_maximum_fusion), slice={[0:2], [0:34], [1:129], [0:258]} | slice | bytes 17965056 | tf_op jit(solution)/shard_map/slice | solution.py:63
  101.1 2.2 broadcast_select_fusion.3
  103.3 2.2 broadcast_select_fusion
  105.5 11.4 %pad_maximum_fusion.1 = f32[2,34,130,258]{3,2,1,0:T(8,128)} fusion(f32[2,34,1,258]{3,2,1,0:T(1,128)S(1)} %broadcast_select_fusion, f32[2,34,128,258]{3,2,1,0:T(8,128)} %slice.148, f32[2,34,1,258]{3,2,1,0:T(1,128)S(1)} %broadcast_select_fusion.3), kind=kLoop, calls=%fused_computation.2 | loop fusion | flops 4561440 | bytes 18245760 | tf_op jit(solution)/shard_map/concatenate | solution.py:68
  116.9 7.5 %slice.151 = f32[2,34,130,256]{3,2,1,0:T(8,128)S(1)} slice(f32[2,34,130,258]{3,2,1,0:T(8,128)} %pad_maximum_fusion.1), slice={[0:2], [0:34], [0:130], [1:257]} | slice | bytes 18104320 | tf_op jit(solution)/shard_map/slice | solution.py:63
  124.4 8.1 %slice_select_fusion.1 = (f32[2,34,130,1]{3,2,1,0:T(8,128)S(1)}, f32[2,34,130,1]{3,2,1,0:T(8,128)S(1)}) fusion(f32[2,34,130,258]{3,2,1,0:T(8,128)} %pad_maximum_fusion.1, pred[]{:T(512)S(6)} %eq.18, pred[]{:T(512)S(6)} %eq.23), kind=kLoop, calls=%fused_computation.12 | loop fusion | flops 17680 | bytes 212162 | tf_op jit(solution)/shard_map/jit(_where)/select_n | solution.py:66
  132.5 8.6 %pad_maximum_fusion.2 = f32[2,34,130,258]{3,2,1,0:T(8,128)} fusion(f32[2,34,130,1]{3,2,1,0:T(8,128)S(1)} %get-tuple-element.44, f32[2,34,130,256]{3,2,1,0:T(8,128)S(1)} %slice.151, f32[2,34,130,1]{3,2,1,0:T(8,128)S(1)} %get-tuple-element.43), kind=kLoop, calls=%fused_computation.3 | loop fusion | flops 4561440 | bytes 18245760 | tf_op jit(solution)/shard_map/concatenate | solution.py:68
  141.1 11.1 %slice_bitcast_fusion = (f32[34,130,258]{2,1,0:T(8,128)}, f32[34,130,258]{2,1,0:T(8,128)}) fusion(f32[2,34,130,258]{3,2,1,0:T(8,128)} %pad_maximum_fusion.2), kind=kLoop, calls=%fused_computation.6 | loop fusion | bytes 18245760 | tf_op jit(solution)/shard_map/squeeze | solution.py:40
  152.2 20.9 %fusion.18 = (f32[128,256]{1,0:T(8,128)}, f32[32,128,256]{2,1,0:T(8,128)S(1)}) fusion(f32[34,130,258]{2,1,0:T(8,128)} %get-tuple-element.42), kind=kLoop, calls=%fused_computation.56 | loop fusion | flops 17793024 | bytes 33685504 | tf_op jit(solution)/shard_map/reduce_sum | solution.py:84
  173.1 3.0 subtract_multiply_fusion
  176.2 39.6 %fusion.22 = (f32[32,128,256]{2,1,0:T(8,128)S(1)}, f32[32,128,256]{2,1,0:T(8,128)}) fusion(f32[34,130,258]{2,1,0:T(8,128)} %get-tuple-element.41, f32[34,130,258]{2,1,0:T(8,128)} %get-tuple-element.42), kind=kLoop, calls=%fused_computation.59 | loop fusion | flops 37748736 | bytes 62914560 | tf_op jit(solution)/shard_map/slice | solution.py:49
  215.8 5.5 %multiply_reduce_fusion = f32[3,128,256]{2,1,0:T(8,128)S(1)} fusion(f32[32,128,256]{2,1,0:T(8,128)} %get-tuple-element.50, f32[3]{0:T(128)S(1)} %get-tuple-element.52, f32[32,128,256]{2,1,0:T(8,128)S(1)} %get-tuple-element.49, f32[3]{0:T(128)S(1)} %get-tuple-element.51, f32[32,128,256]{2,1,0:T(8,128)S(1)} %copy-done), kind=kLoop, calls=%fused_computation.4 | loop fusion | flops 25067520 | bytes 12976152 | tf_op jit(solution)/shard_map/reduce_sum | solution.py:83
  221.3 3.2 all-gather.3.cloned.1.call-done
  225.5 84.4 %reduce-scatter.2.cloned.1.call-done = f32[4,8,256]{2,1,0:T(8,128)} async-done(((f32[4,128,256]{2,1,0:T(8,128)}), f32[4,8,256]{2,1,0:T(8,128)}) %reduce-scatter.2.cloned.1.call-update) | async-done | bytes 32784 | tf_op jit(solution)/shard_map/reduce_scatter | solution.py:89
  (24 shorter events, 4.4 us)
Async XLA Ops:
  6.5 218.0 %all-gather.3.cloned.1.call-start = ((), (), s32[]{:S(2)}) async-start(), calls=%async_computation.2 | async-start | bytes 2228224 | tf_op jit(solution)/shard_map/all_gather | solution.py:22
  7.8 5.7 %collective-permute-start = (f32[2,32,1,256]{3,2,1,0:T(1,128)S(1)}, f32[2,32,1,256]{3,2,1,0:T(1,128)S(1)}, u32[]{:S(2)}, u32[]{:S(2)}) collective-permute-start(f32[2,32,1,256]{3,2,1,0:T(1,128)S(1)} %get-tuple-element.47), channel_id=1, source_target_pairs={{0,32},{32,64},{64,96},{1,33},{33,65},{65,97},{2,34},{34,66},{66,9... | collective-permute-start | bytes 196616 | tf_op jit(solution)/shard_map/ppermute | solution.py:14
  12.2 5.2 %collective-permute-start.1 = (f32[2,32,1,256]{3,2,1,0:T(1,128)S(1)}, f32[2,32,1,256]{3,2,1,0:T(1,128)S(1)}, u32[]{:S(2)}, u32[]{:S(2)}) collective-permute-start(f32[2,32,1,256]{3,2,1,0:T(1,128)S(1)} %get-tuple-element.48), channel_id=1, source_target_pairs={{32,0},{64,32},{96,64},{33,1},{65,33},{97,65},{34,2},{66,34},{98,6... | collective-permute-start | bytes 196616 | tf_op jit(solution)/shard_map/ppermute | solution.py:15
  30.2 9.2 %collective-permute-start.2 = (f32[2,32,130,1]{2,1,3,0:T(8,128)S(1)}, f32[2,32,130,1]{2,1,3,0:T(8,128)S(1)}, u32[]{:S(2)}, u32[]{:S(2)}) collective-permute-start(f32[2,32,130,1]{2,1,3,0:T(8,128)S(1)} %copy.7), channel_id=1, source_target_pairs={{0,16},{1,17},{2,18},{3,19},{4,20},{5,21},{6,22},{7,23},{8,24},{9,... | collective-permute-start | bytes 99848 | tf_op jit(solution)/shard_map/ppermute | solution.py:14
  35.6 6.7 %collective-permute-start.3 = (f32[2,32,130,1]{2,1,3,0:T(8,128)S(1)}, f32[2,32,130,1]{2,1,3,0:T(8,128)S(1)}, u32[]{:S(2)}, u32[]{:S(2)}) collective-permute-start(f32[2,32,130,1]{2,1,3,0:T(8,128)S(1)} %copy.8), channel_id=1, source_target_pairs={{16,0},{17,1},{18,2},{19,3},{20,4},{21,5},{22,6},{23,7},{24,8},{25... | collective-permute-start | bytes 99848 | tf_op jit(solution)/shard_map/ppermute | solution.py:15
  46.5 12.6 %collective-permute-start.4 = (f32[2,1,130,258]{3,2,1,0:T(8,128)S(1)}, f32[2,1,130,258]{3,2,1,0:T(8,128)S(1)}, u32[]{:S(2)}, u32[]{:S(2)}) collective-permute-start(f32[2,1,130,258]{3,2,1,0:T(8,128)S(1)} %pad_maximum_fusion.5), channel_id=1, source_target_pairs={{0,1},{1,2},{2,3},{3,4},{4,5},{5,6},{6,7},{7,8},{8,9},{9,10},{10,1... | collective-permute-start | bytes 804968 | tf_op jit(solution)/shard_map/ppermute | solution.py:14
  49.7 12.1 %copy-start.2 = (f32[2,3]{1,0:T(2,128)S(1)}, f32[2,3]{1,0:T(2,128)}, u32[]{:S(2)}) copy-start(f32[2,3]{1,0:T(2,128)} %param.5) | copy-start | bytes 76
  60.4 13.6 %collective-permute-start.5 = (f32[2,1,130,258]{3,2,1,0:T(8,128)S(1)}, f32[2,1,130,258]{3,2,1,0:T(8,128)S(1)}, u32[]{:S(2)}, u32[]{:S(2)}) collective-permute-start(f32[2,1,130,258]{3,2,1,0:T(8,128)S(1)} %get-tuple-element.40), channel_id=1, source_target_pairs={{1,0},{2,1},{3,2},{4,3},{5,4},{6,5},{7,6},{8,7},{9,8},{10,9},{11,1... | collective-permute-start | bytes 804968 | tf_op jit(solution)/shard_map/ppermute | solution.py:15
  176.1 133.8 %reduce-scatter.2.cloned.1.call-start = ((), (), s32[]{:S(2)}) async-start(), calls=%async_computation.1 | async-start | bytes 557056 | tf_op jit(solution)/shard_map/reduce_scatter | solution.py:89
  176.2 39.6 %copy-start = (f32[32,128,256]{2,1,0:T(8,128)S(1)}, f32[32,128,256]{2,1,0:T(8,128)}, u32[]{:S(2)}) copy-start(f32[32,128,256]{2,1,0:T(8,128)} %subtract_multiply_fusion) | copy-start | bytes 12582916
  215.8 8.8 %copy-start.1 = (f32[128,256]{1,0:T(8,128)S(1)}, f32[128,256]{1,0:T(8,128)}, u32[]{:S(2)}) copy-start(f32[128,256]{1,0:T(8,128)} %get-tuple-element.37) | copy-start | bytes 393220
Sparse Core Ops, SparseCore 0:
  176.3 48.1 all-gather.2
  227.7 82.2 reduce-scatter.1
where the time goes:
time: 321 us; the launch traced here: 319 us
  other arithmetic  126 us (39%)
  waiting for transfers between devices  113 us (35%)
  local copies, waits for them, and re-layouts  51.2 us (16%)
  starting transfers between devices  15.5 us (5%)
  between operations  13.6 us (4%)
    reduce_scatter x1, waiting for transfers between devices, body(): summed = lax.psum_scatter(weighted, 'gz', scatter_dimension=1, tiled=True)  84.4 us
    slice x1, other arithmetic, shade(): heat_inner = heat[1:-1, 1:-1, 1:-1]  39.6 us
    concatenate x3, other arithmetic, clamp_edges(): return jnp.concatenate([lower, middle, upper], axis=dim_pos)  35.1 us
    reduce_sum x1, other arithmetic, body(): brick_depth = jnp.sum(optical, axis=0)  20.9 us
    slice x2, local copies, waits for them, and re-layouts, clamp_edges(): middle = lax.slice_in_dim(padded, 1, length - 1, axis=dim_pos)  19.4 us
    ppermute x3, waiting for transfers between devices, padded_2(): after = lax.ppermute(leading, axis, down)  15.9 us
    select_n x3, other arithmetic, clamp_edges(): lower = jnp.where(place == 0, first_layer, lower)  11.5 us
    squeeze x1, local copies, waits for them, and re-layouts, shade(): heat = padded[1]  11.1 us
  transfers between devices with their start and end apart: 8, of which 5 were waited for; matrix products, arithmetic and copies ran while one was open for 16% of the time, Pallas kernels for 0%

commit v1 on v0

v1 whole, which is shorter than its diff:
```python
import functools

import jax
import jax.numpy as jnp
from jax import lax
from jax.experimental import pallas as pl
from jax.experimental.pallas import tpu as pltpu
from jax.sharding import PartitionSpec as P

MESH = pl.DeviceIdType.MESH
F32 = jnp.float32
LANES = 128
ROWS = 8
LOG2E = 1.4426950408889634
C1 = 0.005 * LOG2E
C2 = 0.016 * LOG2E


def cell(dz, dy, dx, s, ez, ey, ex, u, pal, nz, ny):
    r = lax.rsqrt(dz * dz + dy * dy + dx * dx + 4.0)
    depth = jnp.exp2(s * LOG2E) * (C2 * (r * r) - C1)
    face = jnp.abs(nz * dz + ny * dy + dx) * r + 0.3 / 0.56
    around = pltpu.reciprocal(ez * ez + ey * ey + ex * ex + 4.0, approx=True)
    light = face * (0.375 - around)
    tints = [jnp.tanh(pal[0][c] * u + pal[1][c]) for c in range(3)]
    return depth, light, tints


def kernel(
    sizes, lag, lead, group,
    pal_ref, f_ref, o_ref,
    vol, zh, hs, hx, inner, part, recv,
    load_sem, zsend, zrecv, ysend, yrecv, xsend, xrecv, asend, arecv,
):
    n_iy, n_ix, n_gz = sizes
    nz, ny = f_ref.shape[1], f_ref.shape[2]
    nb = n_gz
    ng = nb // group
    iy, ix, g = lax.axis_index("iy"), lax.axis_index("ix"), lax.axis_index("gz")
    sgn = jnp.where(g < nb // 2, 1, -1)
    hh, hc = 1 - ix, ix
    top, bottom = ROWS - 1, ROWS + ny

    def wrap(i, n):
        return lax.rem(i + 2 * n, n)

    def order(i):
        return wrap(g + sgn * (i + 1), nb)

    def rows8(b):
        return pl.ds(pl.multiple_of(ROWS * b, ROWS), ROWS)

    def shifted(b, by):
        return pl.ds(pl.multiple_of(ROWS * b, ROWS) + by, ROWS)

    def load(l, half):
        b = wrap(g + sgn * l, nb)
        return pltpu.make_async_copy(
            f_ref.at[:, :, rows8(b), pl.ds(half * LANES, LANES)],
            vol.at[half, :, :, shifted(b, ROWS), :],
            load_sem.at[l, half],
        )

    def start_load(l, _):
        for half in range(2):
            load(l, half).start()
        return 0

    def wait_load(l):
        for half in range(2):
            load(l, half).wait()

    lax.fori_loop(0, nb, start_load, 0)

    barrier = pltpu.get_barrier_semaphore()

    def greet(j, _):
        pl.semaphore_signal(
            barrier, inc=1, device_id={"gz": wrap(g + j, nb)}, device_id_type=MESH
        )
        return 0

    lax.fori_loop(1, nb, greet, 0)
    pl.semaphore_signal(barrier, inc=1, device_id={"ix": 1 - ix}, device_id_type=MESH)

    @pl.when(iy > 0)
    def _():
        pl.semaphore_signal(barrier, inc=1, device_id={"iy": iy - 1}, device_id_type=MESH)

    @pl.when(iy < n_iy - 1)
    def _():
        pl.semaphore_signal(barrier, inc=1, device_id={"iy": iy + 1}, device_id_type=MESH)

    pl.semaphore_wait(barrier, nb + jnp.where(iy > 0, 1, 0) + jnp.where(iy < n_iy - 1, 1, 0))

    def y_copy(side, half, remote):
        source = 0 if remote == (side == 1) else ny - 1
        src = f_ref.at[:, :, pl.ds(source, 1), pl.ds(half * LANES, LANES)]
        dst = vol.at[half, :, :, pl.ds(bottom if side else top, 1), :]
        if not remote:
            return pltpu.make_async_copy(src, dst, yrecv.at[side, half])
        return pltpu.make_async_remote_copy(
            src, dst, ysend.at[side, half], yrecv.at[side, half],
            device_id={"iy": iy - 1 if side else iy + 1}, device_id_type=MESH,
        )

    def z_rows(q):
        n = ROWS * group
        return pl.ds(pl.multiple_of(q * n, n), n)

    def z_copy(side, q, remote):
        source = 0 if remote == (side == 1) else nz - 1
        src = f_ref.at[:, source, z_rows(q), :]
        dst = zh.at[side, :, z_rows(q), :]
        if not remote:
            return pltpu.make_async_copy(src, dst, zrecv.at[side, q])
        return pltpu.make_async_remote_copy(
            src, dst, zsend.at[side, q], zrecv.at[side, q],
            device_id={"gz": g - 1 if side else g + 1}, device_id_type=MESH,
        )

    def first_group(gg):
        sg = jnp.where(gg < nb // 2, 1, -1)
        return lax.div(wrap(gg + sg, nb), group), sg

    def z_start(j, _):
        @pl.when(g < nb - 1)
        def _():
            q0, sg = first_group(g + 1)
            z_copy(0, wrap(q0 + sg * j, ng), True).start()

        @pl.when(g > 0)
        def _():
            q0, sg = first_group(g - 1)
            z_copy(1, wrap(q0 + sg * j, ng), True).start()

        @pl.when(g == 0)
        def _():
            z_copy(0, j, False).start()

        @pl.when(g == nb - 1)
        def _():
            z_copy(1, j, False).start()

        return 0

    def y_start():
        for half in range(2):
            @pl.when(iy < n_iy - 1)
            def _():
                y_copy(0, half, True).start()

            @pl.when(iy > 0)
            def _():
                y_copy(1, half, True).start()

            @pl.when(iy == 0)
            def _():
                y_copy(0, half, False).start()

            @pl.when(iy == n_iy - 1)
            def _():
                y_copy(1, half, False).start()

    lane = lax.broadcasted_iota(jnp.int32, (ROWS, LANES), 1)
    out_roll = jnp.where(ix == 0, LANES - 1, 1)
    in_roll = LANES - out_roll
    edge = jnp.where(ix == 0, LANES - 1, 0)
    at_edge = lane == edge
    at_inner = lane == LANES - 1 - edge
    nz_dir = jnp.where(ix == 0, 0.45, -0.45).astype(F32)
    ny_dir = jnp.where(ix == 0, 0.6, -0.6).astype(F32)
    pal = [[0.5 * pal_ref[i, c] for c in range(3)] for i in range(2)]

    def pack(b):
        for f in range(2):
            acc = None
            for z in range(nz):
                column = pltpu.roll(
                    vol[hh, f, z, shifted(b, ROWS), :], lax.rem(z - edge + LANES, LANES), 1
                )
                acc = column if acc is None else jnp.where(lane == z, column, acc)
            hs[f, rows8(b), :] = acc

    def x_copy(b):
        return pltpu.make_async_remote_copy(
            hs.at[:, rows8(b), :], hx.at[:, rows8(b), :], xsend.at[b], xrecv.at[b],
            device_id={"ix": 1 - ix}, device_id_type=MESH,
        )

    def a_copy(b, slot):
        return pltpu.make_async_remote_copy(
            part.at[b], recv.at[slot], asend.at[b], arecv.at[slot],
            device_id={"gz": b}, device_id_type=MESH,
        )

    def planes(b, f, z):
        return [vol[half, f, z, shifted(b, ROWS), :] for half in (hc, hh)]

    def layer(b, z, before, now, after):
        diffs = []
        for f in range(2):
            c, h = now[f]
            beside = pltpu.roll(hx[f, rows8(b), :], lax.rem(edge - z + LANES, LANES), 1)
            oc, oh = pltpu.roll(c, out_roll, 1), pltpu.roll(h, out_roll, 1)
            ic, ih = pltpu.roll(c, in_roll, 1), pltpu.roll(h, in_roll, 1)
            dx = [
                jnp.where(at_edge, oh, oc) - jnp.where(at_inner, c, ic),
                jnp.where(at_edge, beside, oh) - jnp.where(at_inner, ic, ih),
            ]
            dy = [
                vol[half, f, z, shifted(b, ROWS + 1), :] - vol[half, f, z, shifted(b, ROWS - 1), :]
                for half in (hc, hh)
            ]
            dz = [after[f][k] - before[f][k] for k in range(2)]
            diffs.append((dz, dy, dx))
        (dz, dy, dx), (ez, ey, ex) = diffs
        return [
            cell(
                dz[k], dy[k], dx[k], now[0][k], ez[k], ey[k], ex[k], now[1][k],
                pal, nz_dir, ny_dir,
            )
            for k in range(2)
        ]

    def interior(b):
        zero, one = jnp.zeros((ROWS, LANES), F32), jnp.ones((ROWS, LANES), F32)
        depth, left = [zero, zero], [one, one]
        sums = [[zero] * 4, [zero] * 4]
        before = [planes(b, f, 0) for f in range(2)]
        now = [planes(b, f, 1) for f in range(2)]
        for z in range(1, nz - 1):
            after = [planes(b, f, z + 1) for f in range(2)]
            for k, (d, light, tints) in enumerate(layer(b, z, before, now, after)):
                depth[k] = depth[k] + d
                still = jnp.exp2(depth[k])
                lit = (left[k] - still) * light
                left[k] = still
                sums[k] = [sums[k][0] + lit] + [
                    sums[k][1 + c] + lit * tints[c] for c in range(3)
                ]
            before, now = now, after
        for k in range(2):
            for c in range(4):
                inner[k, c, rows8(b), :] = sums[k][c]
            inner[k, 4, rows8(b), :] = depth[k]

    def boundary(b, slot, dst):
        def halo(side, f):
            return [
                zh[side, f, rows8(slot), pl.ds(pl.multiple_of(half * LANES, LANES), LANES)]
                for half in (hc, hh)
            ]

        front = layer(
            b, 0, [halo(0, f) for f in range(2)],
            [planes(b, f, 0) for f in range(2)], [planes(b, f, 1) for f in range(2)],
        )
        back = layer(
            b, nz - 1, [planes(b, f, nz - 2) for f in range(2)],
            [planes(b, f, nz - 1) for f in range(2)], [halo(1, f) for f in range(2)],
        )
        for k, half in enumerate((hc, hh)):
            to = pl.ds(pl.multiple_of(half * LANES, LANES), LANES)
            sums = [inner[k, c, rows8(slot), :] for c in range(4)]
            depth = inner[k, 4, rows8(slot), :]
            d0, light0, tints0 = front[k]
            d1, light1, tints1 = back[k]
            t0, t1 = jnp.exp2(d0), jnp.exp2(d0 + depth)
            whole = d0 + depth + d1
            lit0 = (1.0 - t0) * light0
            lit1 = (t1 - jnp.exp2(whole)) * light1
            base = lit0 + t0 * sums[0] + lit1
            for c in range(3):
                tone = lit0 * tints0[c] + t0 * sums[1 + c] + lit1 * tints1[c]
                dst[c, :, to] = 1.12 * (base + tone)
            dst[3, :, to] = whole

    def send(b):
        @pl.when(b != g)
        def _():
            a_copy(b, g).start()

    q0, _ = first_group(g)

    def z_wait(j, b):
        enters = jnp.where(sgn > 0, lax.rem(b, group) == 0, lax.rem(b, group) == group - 1)
        fresh = (j == 0) | (enters & (lax.div(b, group) != q0))

        @pl.when((j >= 0) & fresh)
        def _():
            for side in range(2):
                z_copy(side, lax.div(b, group), False).wait()

    def prologue(j, _):
        wait_load(j + 1)
        b = order(j)

        @pl.when(j == 0)
        def _():
            lax.fori_loop(0, ng, z_start, 0)
            y_start()

        pack(b)
        x_copy(b).start()
        return 0

    wait_load(0)
    lax.fori_loop(0, lead, prologue, 0)

    def step(i, _):
        b, ahead, behind = order(i), order(i + lead), order(i - lag)
        real = i >= lag

        @pl.when(i + lead < nb)
        def _():
            @pl.when(i + lead + 1 < nb)
            def _():
                wait_load(i + lead + 1)

        for side, at in ((0, 0), (1, nb - 1)):
            @pl.when(b == at)
            def _():
                for half in range(2):
                    y_copy(side, half, False).wait()

        x_copy(b).wait_recv()
        z_wait(i - lag, behind)

        @pl.when(i + lead < nb)
        def _():
            pack(ahead)
            x_copy(ahead).start()

        interior(b)

        @pl.when(real)
        def _():
            boundary(behind, behind, part.at[behind])
            send(behind)

        return 0

    lax.fori_loop(0, nb, step, 0)

    def tail(i, _):
        behind = order(i)
        z_wait(i, behind)
        boundary(behind, behind, part.at[behind])
        send(behind)
        return 0

    lax.fori_loop(nb - lag, nb, tail, 0)
    recv[g] = part[g]

    def arrive(j, _):
        k = wrap(g + j, nb)
        a_copy(k, k).wait_recv()
        return 0

    lax.fori_loop(1, nb, arrive, 0)
    ahead = jnp.zeros(recv.shape[2:], F32)
    sums = [jnp.zeros(recv.shape[2:], F32) for _ in range(3)]
    for k in range(nb):
        clear = jnp.exp2(ahead)
        sums = [sums[c] + clear * recv[k, c] for c in range(3)]
        ahead = ahead + recv[k, 3]
    for c in range(3):
        o_ref[c] = sums[c]
    o_ref[3] = 1.0 - jnp.exp2(ahead)

    def sent(j, _):
        a_copy(wrap(g + j, nb), g).wait_send()
        return 0

    lax.fori_loop(1, nb, sent, 0)

    def columns_sent(b, _):
        x_copy(b).wait_send()
        return 0

    lax.fori_loop(0, nb, columns_sent, 0)

    def layers_sent(q, _):
        @pl.when(g < nb - 1)
        def _():
            z_copy(0, q, True).wait_send()

        @pl.when(g > 0)
        def _():
            z_copy(1, q, True).wait_send()

        return 0

    lax.fori_loop(0, ng, layers_sent, 0)
    for half in range(2):
        @pl.when(iy < n_iy - 1)
        def _():
            y_copy(0, half, True).wait_send()

        @pl.when(iy > 0)
        def _():
            y_copy(1, half, True).wait_send()


def body(sizes, fields, palette):
    n_gz = sizes[2]
    _, nz, ny, nx = fields.shape
    group = 4 if n_gz % 4 == 0 and n_gz > 4 else 1
    lag, lead = (4, 2) if n_gz > 4 else (2, 1)
    dma = pltpu.SemaphoreType.DMA
    return pl.pallas_call(
        functools.partial(kernel, sizes, lag, lead, group),
        out_shape=jax.ShapeDtypeStruct((4, ny // n_gz, nx), F32),
        in_specs=[
            pl.BlockSpec(memory_space=pltpu.SMEM),
            pl.BlockSpec(memory_space=pl.ANY),
        ],
        out_specs=pl.BlockSpec(memory_space=pltpu.VMEM),
        scratch_shapes=[
            pltpu.VMEM((2, 2, nz, ny + 2 * ROWS, LANES), F32),
            pltpu.VMEM((2, 2, ny, nx), F32),
            pltpu.VMEM((2, ny, LANES), F32),
            pltpu.VMEM((2, ny, LANES), F32),
            pltpu.VMEM((2, 5, ny, LANES), F32),
            pltpu.VMEM((n_gz, 4, ROWS, nx), F32),
            pltpu.VMEM((n_gz, 4, ROWS, nx), F32),
            dma((n_gz, 2)),
            dma((2, n_gz // group)),
            dma((2, n_gz // group)),
            dma((2, 2)),
            dma((2, 2)),
            dma((n_gz,)),
            dma((n_gz,)),
            dma((n_gz,)),
            dma((n_gz,)),
        ],
        compiler_params=pltpu.CompilerParams(
            collective_id=0, has_side_effects=True, vmem_limit_bytes=40 << 20
        ),
    )(palette, fields)


def solution(mesh):
    sizes = tuple(mesh.shape[axis] for axis in ("iy", "ix", "gz"))
    return jax.shard_map(
        functools.partial(body, sizes),
        mesh=mesh,
        in_specs=(P(None, "gz", "iy", "ix"), P()),
        out_specs=P(None, ("iy", "gz"), "ix"),
        check_vma=False,
    )
```

time: 321 us -> 35.8 us (0.11)
  other arithmetic: 126 us -> 0 us
  waiting for transfers between devices: 113 us -> 0 us
  local copies, waits for them, and re-layouts: 51.2 us -> 4.68 us
  Pallas kernels: 0 us -> 31 us
  starting transfers between devices: 15.5 us -> 0 us
  between operations: 13.6 us -> 0.01 us
    reduce_scatter x1 -> x0, waiting for transfers between devices: 84.4 us -> none  [body(): summed = lax.psum_scatter(weighted, 'gz', scatter_dimension=1, tiled=True)]
    concatenate x7 -> x0, other arithmetic: 41.9 us -> none  [the longest x3 35.1 us: clamp_edges(): return jnp.concatenate([lower, middle, upper], axis=dim_pos)]
    slice x1 -> x0, other arithmetic: 39.6 us -> none  [shade(): heat_inner = heat[1:-1, 1:-1, 1:-1]]
    slice x7 -> x0, local copies, waits for them, and re-layouts: 34.4 us -> none  [the longest x2 19.4 us: clamp_edges(): middle = lax.slice_in_dim(padded, 1, length - 1, axis=dim_pos)]
    pallas_call x0 -> x1, Pallas kernels: none -> 31 us  [body(): pl.pallas_call(functools.partial(kernel, sizes, lag, lead, group), out_sh...]
    reduce_sum x2 -> x0, other arithmetic: 26.5 us -> none  [the longest x1 20.9 us: body(): brick_depth = jnp.sum(optical, axis=0)]
    ppermute x6 -> x0, waiting for transfers between devices: 25.2 us -> none  [the longest x3 15.9 us: padded_2(): after = lax.ppermute(leading, axis, down)]
    ppermute x6 -> x0, starting transfers between devices: 15.5 us -> none  [the longest x3 8.89 us: padded_2(): before = lax.ppermute(last, axis, up)]
  transfers between devices with their start and end apart: 8 -> 0, of which waited for: 5 -> 0; matrix products, arithmetic and copies ran while one was open for 16% -> 0% of each run, Pallas kernels for 0% -> 0%
where the time goes in v1:
time: 35.8 us; the launch traced here: 35.7 us
  Pallas kernels  31 us (87%)
  local copies, waits for them, and re-layouts  4.68 us (13%)
    pallas_call x1, Pallas kernels, body(): pl.pallas_call(functools.partial(kernel, sizes, lag, lead, group), out_sh...  31 us
    unnamed x5, local copies, waits for them, and re-layouts  4.68 us

profile of v1, /device:TPU:1, one launch (start us, length us, event | category | flops | bytes accessed | tf_op | source)
XLA Modules:
  0.0 35.7 jit_solution(14226579099966136768)
XLA Ops:
  0.0 0.0 copy-start
  0.0 3.4 %copy-done = f32[2,32,128,256]{3,2,1,0:T(8,128)S(1)} copy-done((f32[2,32,128,256]{3,2,1,0:T(8,128)S(1)}, f32[2,32,128,256]{3,2,1,0:T(8,128)}, u32[]{:S(2)}) %copy-start) | copy-done | bytes 8388632
  3.4 0.0 copy-start.1
  3.4 0.7 %copy-done.1 = f32[2,3]{1,0:T(2,128)S(1)} copy-done((f32[2,3]{1,0:T(2,128)S(1)}, f32[2,3]{1,0:T(2,128)}, u32[]{:S(2)}) %copy-start.1) | copy-done | bytes 48
  4.1 31.0 %shard_map.28 = f32[4,8,256]{2,1,0:T(8,128)S(1)} custom-call(f32[2,3]{1,0:T(2,128)S(1)} %copy-done.1, f32[2,32,128,256]{3,2,1,0:T(8,128)S(1)} %copy-done), custom_call_target="tpu_custom_call" | custom-call | tf_op jit(solution)/shard_map/pallas_call | solution.py:412
  35.1 0.6 %copy.4 = f32[4,8,256]{2,1,0:T(8,128)} copy(f32[4,8,256]{2,1,0:T(8,128)S(1)} %shard_map.28) | data formatting | bytes 65536
Async XLA Ops:
  0.0 3.4 %copy-start = (f32[2,32,128,256]{3,2,1,0:T(8,128)S(1)}, f32[2,32,128,256]{3,2,1,0:T(8,128)}, u32[]{:S(2)}) copy-start(f32[2,32,128,256]{3,2,1,0:T(8,128)} %f_ref.1) | copy-start | bytes 25165828
  3.4 0.7 %copy-start.1 = (f32[2,3]{1,0:T(2,128)S(1)}, f32[2,3]{1,0:T(2,128)}, u32[]{:S(2)}) copy-start(f32[2,3]{1,0:T(2,128)} %pal_ref.1) | copy-start | bytes 76

commit v2 on v1

--- a/solution.py
+++ b/solution.py
@@ -27,10 +27,10 @@
 
 
 def kernel(
-    sizes, lag, lead, group,
-    pal_ref, f_ref, o_ref,
-    vol, zh, hs, hx, inner, part, recv,
-    load_sem, zsend, zrecv, ysend, yrecv, xsend, xrecv, asend, arecv,
+    sizes, early, lead, group,
+    p_ref, f_ref, o_ref,
+    pal_ref, vol, zh, hs, hx, inner, part, recv,
+    pal_sem, load_sem, zsend, zrecv, ysend, yrecv, xsend, xrecv, asend, arecv,
 ):
     n_iy, n_ix, n_gz = sizes
     nz, ny = f_ref.shape[1], f_ref.shape[2]
@@ -70,7 +70,9 @@
         for half in range(2):
             load(l, half).wait()
 
-    lax.fori_loop(0, nb, start_load, 0)
+    colors = pltpu.make_async_copy(p_ref, pal_ref, pal_sem)
+    colors.start()
+    lax.fori_loop(0, lead + 2, start_load, 0)
 
     barrier = pltpu.get_barrier_semaphore()
 
@@ -91,7 +93,7 @@
     def _():
         pl.semaphore_signal(barrier, inc=1, device_id={"iy": iy + 1}, device_id_type=MESH)
 
-    pl.semaphore_wait(barrier, nb + jnp.where(iy > 0, 1, 0) + jnp.where(iy < n_iy - 1, 1, 0))
+    lax.fori_loop(lead + 2, nb, start_load, 0)
 
     def y_copy(side, half, remote):
         source = 0 if remote == (side == 1) else ny - 1
@@ -170,9 +172,10 @@
     at_inner = lane == LANES - 1 - edge
     nz_dir = jnp.where(ix == 0, 0.45, -0.45).astype(F32)
     ny_dir = jnp.where(ix == 0, 0.6, -0.6).astype(F32)
+    colors.wait()
     pal = [[0.5 * pal_ref[i, c] for c in range(3)] for i in range(2)]
 
-    def pack(b):
+    def pack(b, slot):
         for f in range(2):
             acc = None
             for z in range(nz):
@@ -180,7 +183,7 @@
                     vol[hh, f, z, shifted(b, ROWS), :], lax.rem(z - edge + LANES, LANES), 1
                 )
                 acc = column if acc is None else jnp.where(lane == z, column, acc)
-            hs[f, rows8(b), :] = acc
+            hs[f, rows8(slot), :] = acc
 
     def x_copy(b):
         return pltpu.make_async_remote_copy(
@@ -223,14 +226,25 @@
             for k in range(2)
         ]
 
-    def interior(b):
+    def halo(b, side, f):
+        return [
+            zh[side, f, rows8(b), pl.ds(pl.multiple_of(half * LANES, LANES), LANES)]
+            for half in (hc, hh)
+        ]
+
+    def render(b, first, last):
         zero, one = jnp.zeros((ROWS, LANES), F32), jnp.ones((ROWS, LANES), F32)
         depth, left = [zero, zero], [one, one]
         sums = [[zero] * 4, [zero] * 4]
-        before = [planes(b, f, 0) for f in range(2)]
-        now = [planes(b, f, 1) for f in range(2)]
-        for z in range(1, nz - 1):
-            after = [planes(b, f, z + 1) for f in range(2)]
+
+        def plane(z):
+            if z < 0 or z >= nz:
+                return [halo(b, 0 if z < 0 else 1, f) for f in range(2)]
+            return [planes(b, f, z) for f in range(2)]
+
+        before, now = plane(first - 1), plane(first)
+        for z in range(first, last + 1):
+            after = plane(z + 1)
             for k, (d, light, tints) in enumerate(layer(b, z, before, now, after)):
                 depth[k] = depth[k] + d
                 still = jnp.exp2(depth[k])
@@ -240,41 +254,45 @@
                     sums[k][1 + c] + lit * tints[c] for c in range(3)
                 ]
             before, now = now, after
+        return sums, depth
+
+    def interior(b, i):
+        sums, depth = render(b, 1, nz - 2)
         for k in range(2):
             for c in range(4):
-                inner[k, c, rows8(b), :] = sums[k][c]
-            inner[k, 4, rows8(b), :] = depth[k]
-
-    def boundary(b, slot, dst):
-        def halo(side, f):
-            return [
-                zh[side, f, rows8(slot), pl.ds(pl.multiple_of(half * LANES, LANES), LANES)]
-                for half in (hc, hh)
-            ]
-
+                inner[i, k, c] = sums[k][c]
+            inner[i, k, 4] = depth[k]
+
+    def boundary(b, i):
         front = layer(
-            b, 0, [halo(0, f) for f in range(2)],
+            b, 0, [halo(b, 0, f) for f in range(2)],
             [planes(b, f, 0) for f in range(2)], [planes(b, f, 1) for f in range(2)],
         )
         back = layer(
             b, nz - 1, [planes(b, f, nz - 2) for f in range(2)],
-            [planes(b, f, nz - 1) for f in range(2)], [halo(1, f) for f in range(2)],
+            [planes(b, f, nz - 1) for f in range(2)], [halo(b, 1, f) for f in range(2)],
         )
         for k, half in enumerate((hc, hh)):
-            to = pl.ds(pl.multiple_of(half * LANES, LANES), LANES)
-            sums = [inner[k, c, rows8(slot), :] for c in range(4)]
-            depth = inner[k, 4, rows8(slot), :]
+            sums = [inner[i, k, c] for c in range(4)]
+            depth = inner[i, k, 4]
             d0, light0, tints0 = front[k]
             d1, light1, tints1 = back[k]
             t0, t1 = jnp.exp2(d0), jnp.exp2(d0 + depth)
             whole = d0 + depth + d1
             lit0 = (1.0 - t0) * light0
             lit1 = (t1 - jnp.exp2(whole)) * light1
-            base = lit0 + t0 * sums[0] + lit1
-            for c in range(3):
-                tone = lit0 * tints0[c] + t0 * sums[1 + c] + lit1 * tints1[c]
-                dst[c, :, to] = 1.12 * (base + tone)
-            dst[3, :, to] = whole
+            keep(
+                b, half,
+                [lit0 + t0 * sums[0] + lit1]
+                + [lit0 * tints0[c] + t0 * sums[1 + c] + lit1 * tints1[c] for c in range(3)],
+                whole,
+            )
+
+    def keep(b, half, sums, depth):
+        to = pl.ds(pl.multiple_of(half * LANES, LANES), LANES)
+        for c in range(3):
+            part[b, c, :, to] = 1.12 * (sums[0] + sums[1 + c])
+        part[b, 3, :, to] = depth
 
     def send(b):
         @pl.when(b != g)
@@ -292,31 +310,22 @@
             for side in range(2):
                 z_copy(side, lax.div(b, group), False).wait()
 
-    def prologue(j, _):
-        wait_load(j + 1)
-        b = order(j)
-
-        @pl.when(j == 0)
-        def _():
-            lax.fori_loop(0, ng, z_start, 0)
-            y_start()
-
-        pack(b)
-        x_copy(b).start()
-        return 0
-
-    wait_load(0)
-    lax.fori_loop(0, lead, prologue, 0)
-
-    def step(i, _):
-        b, ahead, behind = order(i), order(i + lead), order(i - lag)
-        real = i >= lag
-
-        @pl.when(i + lead < nb)
-        def _():
-            @pl.when(i + lead + 1 < nb)
-            def _():
-                wait_load(i + lead + 1)
+    for l in range(lead + 1):
+        wait_load(l)
+    for j in range(lead):
+        pack(order(j), order(j))
+    pl.semaphore_wait(barrier, nb + jnp.where(iy > 0, 1, 0) + jnp.where(iy < n_iy - 1, 1, 0))
+    for j in range(lead):
+        x_copy(order(j)).start()
+    lax.fori_loop(0, ng, z_start, 0)
+    y_start()
+
+    def wait_step(i):
+        b = order(i)
+
+        @pl.when(i + lead + 1 < nb)
+        def _():
+            wait_load(i + lead + 1)
 
         for side, at in ((0, 0), (1, nb - 1)):
             @pl.when(b == at)
@@ -325,33 +334,78 @@
                     y_copy(side, half, False).wait()
 
         x_copy(b).wait_recv()
-        z_wait(i - lag, behind)
-
+        return b
+
+    def pack_ahead(i):
+        ahead = order(jnp.minimum(i + lead, nb - 1))
+        pack(ahead, jnp.where(i + lead < nb, ahead, nb))
+
+    def send_ahead(i):
         @pl.when(i + lead < nb)
         def _():
-            pack(ahead)
-            x_copy(ahead).start()
-
-        interior(b)
-
-        @pl.when(real)
-        def _():
-            boundary(behind, behind, part.at[behind])
-            send(behind)
-
-        return 0
-
-    lax.fori_loop(0, nb, step, 0)
-
-    def tail(i, _):
-        behind = order(i)
-        z_wait(i, behind)
-        boundary(behind, behind, part.at[behind])
-        send(behind)
-        return 0
-
-    lax.fori_loop(nb - lag, nb, tail, 0)
+            x_copy(order(i + lead)).start()
+
+    def early_step(i, _):
+        b = wait_step(i)
+        pack_ahead(i)
+        interior(b, i)
+        send_ahead(i)
+        return 0
+
+    lax.fori_loop(0, early, early_step, 0)
+    for i in range(early):
+        z_wait(i, order(i))
+    for i in range(early):
+        boundary(order(i), i)
+    for i in range(early):
+        send(order(i))
+
+    def late_step(i, _):
+        b = wait_step(i)
+        z_wait(i, b)
+        pack_ahead(i)
+        sums, depth = render(b, 0, nz - 1)
+        for k, half in enumerate((hc, hh)):
+            keep(b, half, sums[k], depth[k])
+        send_ahead(i)
+        send(b)
+        return 0
+
+    lax.fori_loop(early, nb, late_step, 0)
     recv[g] = part[g]
+
+    def sent(j, _):
+        a_copy(wrap(g + j, nb), g).wait_send()
+        return 0
+
+    lax.fori_loop(1, nb, sent, 0)
+
+    def columns_sent(b, _):
+        x_copy(b).wait_send()
+        return 0
+
+    lax.fori_loop(0, nb, columns_sent, 0)
+
+    def layers_sent(q, _):
+        @pl.when(g < nb - 1)
+        def _():
+            z_copy(0, q, True).wait_send()
+
+        @pl.when(g > 0)
+        def _():
+            z_copy(1, q, True).wait_send()
+
+        return 0
+
+    lax.fori_loop(0, ng, layers_sent, 0)
+    for half in range(2):
+        @pl.when(iy < n_iy - 1)
+        def _():
+            y_copy(0, half, True).wait_send()
+
+        @pl.when(iy > 0)
+        def _():
+            y_copy(1, half, True).wait_send()
 
     def arrive(j, _):
         k = wrap(g + j, nb)
@@ -369,62 +423,31 @@
         o_ref[c] = sums[c]
     o_ref[3] = 1.0 - jnp.exp2(ahead)
 
-    def sent(j, _):
-        a_copy(wrap(g + j, nb), g).wait_send()
-        return 0
-
-    lax.fori_loop(1, nb, sent, 0)
-
-    def columns_sent(b, _):
-        x_copy(b).wait_send()
-        return 0
-
-    lax.fori_loop(0, nb, columns_sent, 0)
-
-    def layers_sent(q, _):
-        @pl.when(g < nb - 1)
-        def _():
-            z_copy(0, q, True).wait_send()
-
-        @pl.when(g > 0)
-        def _():
-            z_copy(1, q, True).wait_send()
-
-        return 0
-
-    lax.fori_loop(0, ng, layers_sent, 0)
-    for half in range(2):
-        @pl.when(iy < n_iy - 1)
-        def _():
-            y_copy(0, half, True).wait_send()
-
-        @pl.when(iy > 0)
-        def _():
-            y_copy(1, half, True).wait_send()
-
 
 def body(sizes, fields, palette):
     n_gz = sizes[2]
     _, nz, ny, nx = fields.shape
     group = 4 if n_gz % 4 == 0 and n_gz > 4 else 1
-    lag, lead = (4, 2) if n_gz > 4 else (2, 1)
+    early, lead = (6, 4) if n_gz > 4 else (2, 1)
     dma = pltpu.SemaphoreType.DMA
     return pl.pallas_call(
-        functools.partial(kernel, sizes, lag, lead, group),
+        functools.partial(kernel, sizes, early, lead, group),
         out_shape=jax.ShapeDtypeStruct((4, ny // n_gz, nx), F32),
         in_specs=[
-            pl.BlockSpec(memory_space=pltpu.SMEM),
+            pl.BlockSpec(memory_space=pl.ANY),
             pl.BlockSpec(memory_space=pl.ANY),
         ],
         out_specs=pl.BlockSpec(memory_space=pltpu.VMEM),
         scratch_shapes=[
+            pltpu.SMEM((2, 3), F32),
             pltpu.VMEM((2, 2, nz, ny + 2 * ROWS, LANES), F32),
             pltpu.VMEM((2, 2, ny, nx), F32),
+            pltpu.VMEM((2, ny + ROWS, LANES), F32),
             pltpu.VMEM((2, ny, LANES), F32),
-            pltpu.VMEM((2, ny, LANES), F32),
-            pltpu.VMEM((2, 5, ny, LANES), F32),
+            pltpu.VMEM((early, 2, 5, ROWS, LANES), F32),
             pltpu.VMEM((n_gz, 4, ROWS, nx), F32),
             pltpu.VMEM((n_gz, 4, ROWS, nx), F32),
+            dma(()),
             dma((n_gz, 2)),
             dma((2, n_gz // group)),
             dma((2, n_gz // group)),
@@ -436,7 +459,7 @@
             dma((n_gz,)),
         ],
         compiler_params=pltpu.CompilerParams(
-            collective_id=0, has_side_effects=True, vmem_limit_bytes=40 << 20
+            collective_id=0, has_side_effects=True, vmem_limit_bytes=60 << 20
         ),
     )(palette, fields)
 

time: 35.8 us -> 26.5 us (0.74)
  Pallas kernels: 31 us -> 24.9 us
  local copies, waits for them, and re-layouts: 4.68 us -> 1.38 us
    pallas_call x1, Pallas kernels: 31 us -> 24.9 us  [body(): pl.pallas_call(functools.partial(kernel, sizes, early, lead, group), out_...]
    unnamed x5 -> x1, local copies, waits for them, and re-layouts: 4.68 us -> 1.38 us
where the time goes in v2:
time: 26.5 us; the launch traced here: 26.3 us
  Pallas kernels  24.9 us (94%)
  local copies, waits for them, and re-layouts  1.38 us (5%)
    pallas_call x1, Pallas kernels, body(): pl.pallas_call(functools.partial(kernel, sizes, early, lead, group), out_...  24.9 us
    unnamed x1, local copies, waits for them, and re-layouts  1.38 us

profile of v2, /device:TPU:1, one launch (start us, length us, event | category | flops | bytes accessed | tf_op | source)
XLA Modules:
  0.0 26.3 jit_solution(13704049013531084433)
XLA Ops:
  0.0 24.9 %shard_map.28 = f32[4,8,256]{2,1,0:T(8,128)} custom-call(f32[2,3]{1,0:T(2,128)} %p_ref.1, f32[2,32,128,256]{3,2,1,0:T(8,128)} %f_ref.1), custom_call_target="tpu_custom_call" | custom-call | tf_op jit(solution)/shard_map/pallas_call | solution.py:433
  25.0 1.4 %copy.4 = f32[4,8,256]{2,1,0:T(8,128)} copy(f32[4,8,256]{2,1,0:T(8,128)} %shard_map.28) | data formatting | bytes 65536

commit v3 on v1

v3 whole, which is shorter than its diff:
```python
import functools

import jax
import jax.numpy as jnp
from jax import lax
from jax.experimental import pallas as pl
from jax.experimental.pallas import tpu as pltpu
from jax.sharding import PartitionSpec as P

MESH = pl.DeviceIdType.MESH
F32 = jnp.float32
LANES = 128
ROWS = 8
LOG2E = 1.4426950408889634
C1 = 0.005 * LOG2E
C2 = 0.016 * LOG2E


def cell(dz, dy, dx, s, ez, ey, ex, u, pal, nz, ny):
    r = lax.rsqrt(dz * dz + dy * dy + dx * dx + 4.0)
    depth = jnp.exp2(s * LOG2E) * (C2 * (r * r) - C1)
    face = jnp.abs(nz * dz + ny * dy + dx) * r + 0.3 / 0.56
    around = pltpu.reciprocal(ez * ez + ey * ey + ex * ex + 4.0, approx=True)
    light = face * (0.375 - around)
    tints = [jnp.tanh(pal[0][c] * u + pal[1][c]) for c in range(3)]
    return depth, light, tints


def kernel(
    sizes, gap, entry, pair,
    p_ref, f_ref, o_ref,
    pal_ref, vol, zh, hs, hx, outs, ins, inner, part, recv,
    pal_sem, all_sem, load_sem, zsend, zrecv, ysend, yrecv, xsend, xrecv, asend, arecv,
):
    n_iy, n_ix, n_gz = sizes
    nz, ny = f_ref.shape[1], f_ref.shape[2]
    nb = n_gz
    iy, ix, g = lax.axis_index("iy"), lax.axis_index("ix"), lax.axis_index("gz")
    sgn = jnp.where(g < nb // 2, 1, -1)
    hh, hc = 1 - ix, ix
    top, bottom = ROWS - 1, ROWS + ny

    def wrap(i, n):
        return lax.rem(i + 2 * n, n)

    def order(i):
        return wrap(g + sgn * (i + 1), nb)

    ring = 4 if nb > 4 else nb
    cols = nb // ring
    gx, gy = lax.div(g, ring), lax.rem(g, ring)

    def hops(o):
        dx, dy = o // ring, o % ring
        return min(dx, cols - dx) + min(dy, ring - dy)

    turns = sorted(range(nb), key=lambda o: (-hops(o), -min(o % ring, ring - o % ring), o))

    def far_first(j, gx, gy):
        o = jnp.int32(0)
        for k, turn in enumerate(turns):
            o = o + jnp.where(j == k, turn, 0)
        return wrap(gx + lax.div(o, ring), cols) * ring + wrap(gy + lax.rem(o, ring), ring)

    def rows8(b):
        return pl.ds(pl.multiple_of(ROWS * b, ROWS), ROWS)

    def shifted(b, by):
        return pl.ds(pl.multiple_of(ROWS * b, ROWS) + by, ROWS)

    def load(l, half):
        b = wrap(g + sgn * l, nb)
        return pltpu.make_async_copy(
            f_ref.at[:, :, rows8(b), pl.ds(half * LANES, LANES)],
            vol.at[half, :, :, shifted(b, ROWS), :],
            load_sem.at[l],
        )

    def start_load(l, _):
        for half in range(2):
            load(l, half).start()
        return 0

    def landed(ref, sem):
        pltpu.make_async_copy(ref, ref, sem).wait()

    def wait_load(l):
        landed(vol.at[:, :, :, pl.ds(ROWS, ROWS), :], load_sem.at[l])

    colors = pltpu.make_async_copy(p_ref, pal_ref, pal_sem)
    colors.start()
    lax.fori_loop(0, pair + 2, start_load, 0)

    barrier = pltpu.get_barrier_semaphore()

    def to_row(j):
        return {"gz": gx * ring + wrap(gy + j, ring)}

    def to_col(j):
        return {"gz": wrap(gx + j, cols) * ring + gy}

    def hello(sem, where):
        pl.semaphore_signal(sem, inc=1, device_id=where, device_id_type=MESH)

    skew_up = (gy == ring - 1) & (g < nb - 1)
    skew_down = (gy == 0) & (g > 0)

    hello(barrier, {"ix": 1 - ix})
    for there, where in (
        (iy > 0, {"iy": iy - 1}),
        (iy < n_iy - 1, {"iy": iy + 1}),
        (skew_up, {"gz": g + 1}),
        (skew_down, {"gz": g - 1}),
    ):
        @pl.when(there)
        def _(where=where):
            hello(barrier, where)
    for j in range(1, ring):
        hello(barrier, to_row(j))
    for j in range(1, cols):
        hello(barrier, to_col(j))
    beside = 1 + (ring - 1) + (cols - 1)
    for there in (iy > 0, iy < n_iy - 1, skew_up, skew_down):
        beside = beside + jnp.where(there, 1, 0)

    lax.fori_loop(pair + 2, nb, start_load, 0)

    def y_copy(side, half, remote):
        source = 0 if remote == (side == 1) else ny - 1
        src = f_ref.at[:, :, pl.ds(source, 1), pl.ds(half * LANES, LANES)]
        dst = vol.at[half, :, :, pl.ds(bottom if side else top, 1), :]
        if not remote:
            return pltpu.make_async_copy(src, dst, yrecv.at[side])
        return pltpu.make_async_remote_copy(
            src, dst, ysend.at[side], yrecv.at[side],
            device_id={"iy": iy - 1 if side else iy + 1}, device_id_type=MESH,
        )

    def z_copy(side, b, remote):
        source = 0 if remote == (side == 1) else nz - 1
        src = f_ref.at[:, source, rows8(b), :]
        dst = zh.at[side, :, rows8(b), :]
        if not remote:
            return pltpu.make_async_copy(src, dst, zrecv.at[b])
        return pltpu.make_async_remote_copy(
            src, dst, zsend.at[side], zrecv.at[b],
            device_id={"gz": g - 1 if side else g + 1}, device_id_type=MESH,
        )

    def z_start(j, _):
        @pl.when(g < nb - 1)
        def _():
            z_copy(0, far_first(j, lax.div(g + 1, ring), lax.rem(g + 1, ring)), True).start()

        @pl.when(g > 0)
        def _():
            z_copy(1, far_first(j, lax.div(g - 1, ring), lax.rem(g - 1, ring)), True).start()

        @pl.when(g == 0)
        def _():
            z_copy(0, j, False).start()

        @pl.when(g == nb - 1)
        def _():
            z_copy(1, j, False).start()

        return 0

    def y_start():
        for half in range(2):
            @pl.when(iy < n_iy - 1)
            def _():
                y_copy(0, half, True).start()

            @pl.when(iy > 0)
            def _():
                y_copy(1, half, True).start()

            @pl.when(iy == 0)
            def _():
                y_copy(0, half, False).start()

            @pl.when(iy == n_iy - 1)
            def _():
                y_copy(1, half, False).start()

    lane = lax.broadcasted_iota(jnp.int32, (ROWS, LANES), 1)
    out_roll = jnp.where(ix == 0, LANES - 1, 1)
    in_roll = LANES - out_roll
    edge = jnp.where(ix == 0, LANES - 1, 0)
    at_edge = lane == edge
    at_inner = lane == LANES - 1 - edge
    nz_dir = jnp.where(ix == 0, 0.45, -0.45).astype(F32)
    ny_dir = jnp.where(ix == 0, 0.6, -0.6).astype(F32)
    colors.wait()
    pal = [[0.5 * pal_ref[i, c] for c in range(3)] for i in range(2)]

    def spread(z, side):
        return 2 * z + 1 if z % 2 == 0 else 2 * z - 1 + side

    def pack(b, f, edges):
        side = jnp.where(ix == 0, -1, 1)
        acc = None
        for z in range(0, nz, 2):
            both = jnp.where(at_edge, edges[z][0], edges[z + 1][1])
            to = spread(z, side)
            both = pltpu.roll(both, lax.rem(to - edge + LANES, LANES), 1)
            acc = both if acc is None else jnp.where(lane >= to - 1, both, acc)
        hs[f, rows8(b), :] = acc

    def x_copy(b):
        return pltpu.make_async_remote_copy(
            hs.at[:, rows8(b), :], hx.at[:, rows8(b), :], xsend, xrecv.at[b],
            device_id={"ix": 1 - ix}, device_id_type=MESH,
        )

    def a_copy(b, slot):
        return pltpu.make_async_remote_copy(
            part.at[b], recv.at[slot], asend, arecv,
            device_id={"gz": b}, device_id_type=MESH,
        )

    def planes(b, f, z):
        return [vol[half, f, z, shifted(b, ROWS), :] for half in (hc, hh)]

    def at(half, f, z, b):
        return vol[half, f, z, shifted(b, ROWS), :]

    def dy_of(half, f, z, b):
        return vol[half, f, z, shifted(b, ROWS + 1), :] - vol[half, f, z, shifted(b, ROWS - 1), :]

    def beyond(side, f, half, b):
        return zh[side, f, rows8(b), pl.ds(pl.multiple_of(half * LANES, LANES), LANES)]

    def column(half, f, z, b):
        if z < 0:
            return beyond(0, f, half, b)
        if z >= nz:
            return beyond(1, f, half, b)
        return at(half, f, z, b)

    def dz_of(half, f, z, b):
        return column(half, f, z + 1, b) - column(half, f, z - 1, b)

    def inner_dx(f, z, b, now, out):
        inward = pltpu.roll(now, in_roll, 1)
        dx = jnp.where(at_edge, out, pltpu.roll(now, out_roll, 1)) - jnp.where(at_inner, now, inward)
        return dx, inward

    def outer_dx(f, z, b, now, out, inward):
        side = jnp.where(ix == 0, 1, -1)
        beside = pltpu.roll(hx[f, rows8(b), :], lax.rem(edge - spread(z, side) + LANES, LANES), 1)
        return jnp.where(at_edge, beside, out) - jnp.where(at_inner, inward, pltpu.roll(now, in_roll, 1))

    def shade(half, z, b, now, dx):
        dz = [dz_of(half, f, z, b) for f in range(2)]
        dy = [dy_of(half, f, z, b) for f in range(2)]
        return cell(
            dz[0], dy[0], dx[0], now[0], dz[1], dy[1], dx[1], now[1], pal, nz_dir, ny_dir
        )

    def clean():
        zero, one = jnp.zeros((ROWS, LANES), F32), jnp.ones((ROWS, LANES), F32)
        return [zero, one] + [zero] * 4

    def add(state, d, light, tints):
        depth = state[0] + d
        still = jnp.exp2(depth)
        lit = (state[1] - still) * light
        return [depth, still, state[2] + lit] + [state[3 + c] + lit * tints[c] for c in range(3)]

    def inner_half(blocks):
        states = [clean() for _ in blocks]
        edges = [[[] for _ in range(2)] for _ in blocks]
        for z in range(nz):
            for k, b in enumerate(blocks):
                now, dx = [], []
                for f in range(2):
                    h = at(hh, f, z, b)
                    out = pltpu.roll(h, out_roll, 1)
                    outs[f, z, rows8(b), :] = out
                    edges[k][f].append((h, out))
                    if 0 < z < nz - 1:
                        now.append(at(hc, f, z, b))
                        d, inward = inner_dx(f, z, b, now[f], out)
                        ins[f, z, rows8(b), :] = inward
                        dx.append(d)
                if 0 < z < nz - 1:
                    states[k] = add(states[k], *shade(hc, z, b, now, dx))
        for k, b in enumerate(blocks):
            for f in range(2):
                pack(b, f, edges[k][f])
            for c in range(6):
                inner[b, c] = states[k][c]

    def outer_half(blocks):
        ends = [{} for _ in blocks]
        states = [clean() for _ in blocks]
        for z in range(nz):
            for k, b in enumerate(blocks):
                now = [at(hh, f, z, b) for f in range(2)]
                out = [outs[f, z, rows8(b), :] for f in range(2)]
                if 0 < z < nz - 1:
                    inward = [ins[f, z, rows8(b), :] for f in range(2)]
                else:
                    mine = [at(hc, f, z, b) for f in range(2)]
                    pairs = [inner_dx(f, z, b, mine[f], out[f]) for f in range(2)]
                    inward = [p[1] for p in pairs]
                    ends[k][z] = shade(hc, z, b, mine, [p[0] for p in pairs])
                dx = [outer_dx(f, z, b, now[f], out[f], inward[f]) for f in range(2)]
                states[k] = add(states[k], *shade(hh, z, b, now, dx))
        for k, b in enumerate(blocks):
            keep(b, hh, states[k])
            (d0, light0, tints0), (d1, light1, tints1) = ends[k][0], ends[k][nz - 1]
            mid = [inner[b, c] for c in range(6)]
            t0 = jnp.exp2(d0)
            lit0 = (1.0 - t0) * light0
            depth = d0 + mid[0] + d1
            lit1 = (t0 * mid[1] - jnp.exp2(depth)) * light1
            sums = [lit0 + t0 * mid[2] + lit1] + [
                lit0 * tints0[c] + t0 * mid[3 + c] + lit1 * tints1[c] for c in range(3)
            ]
            keep(b, hc, [depth, None] + sums)

    def keep(b, half, state):
        to = pl.ds(pl.multiple_of(half * LANES, LANES), LANES)
        for c in range(3):
            part[b, c, :, to] = 1.12 * (state[2] + state[3 + c])
        part[b, 3, :, to] = state[0]

    def send(b):
        @pl.when(b != g)
        def _():
            a_copy(b, g).start()

    for l in range(2):
        wait_load(l)

    def enter():
        pl.semaphore_wait(barrier, beside)
        for j in range(1, cols):
            hello(all_sem, to_col(j))
        y_start()

        def columns(i, _):
            x_copy(order(i)).start()
            return 0

        lax.fori_loop(0, entry, columns, 0)
        lax.fori_loop(0, nb, z_start, 0)

    def step(s, _):
        @pl.when(s == entry // pair)
        def _():
            enter()

        i = s * pair

        @pl.when(i < nb)
        def _():
            for k in range(pair):
                @pl.when(i + k + 2 < nb)
                def _():
                    wait_load(i + k + 2)

                for side, row in ((0, 0), (1, nb - 1)):
                    @pl.when(order(i + k) == row)
                    def _():
                        landed(vol.at[:, :, :, pl.ds(0, 1), :], yrecv.at[side])

            inner_half([order(i + k) for k in range(pair)])

            @pl.when(i >= entry)
            def _():
                for k in range(pair):
                    x_copy(order(i + k)).start()

        @pl.when(i == gap)
        def _():
            if cols > 1:
                pl.semaphore_wait(all_sem, cols - 1)

        @pl.when(i >= gap)
        def _():
            j = i - gap
            blocks = [far_first(j + k, gx, gy) for k in range(pair)]
            for k in range(pair):
                x_copy(blocks[k]).wait_recv()
                landed(zh.at[:, :, rows8(blocks[k]), :], zrecv.at[blocks[k]])
            outer_half(blocks)
            for k in range(pair):
                send(blocks[k])

        return 0

    lax.fori_loop(0, (nb + gap) // pair, step, 0)
    recv[g] = part[g]
    landed(hs, xsend)

    @pl.when(g < nb - 1)
    def _():
        landed(zh.at[0], zsend.at[0])

    @pl.when(g > 0)
    def _():
        landed(zh.at[1], zsend.at[1])

    for side, there in ((0, iy < n_iy - 1), (1, iy > 0)):
        @pl.when(there)
        def _(side=side):
            landed(vol.at[:, :, :, pl.ds(0, 1), :], ysend.at[side])

    landed(part.at[pl.ds(0, nb - 1)], asend)
    landed(recv.at[pl.ds(0, nb - 1)], arecv)
    ahead = jnp.zeros(recv.shape[2:], F32)
    sums = [jnp.zeros(recv.shape[2:], F32) for _ in range(3)]
    for k in range(nb):
        clear = jnp.exp2(ahead)
        sums = [sums[c] + clear * recv[k, c] for c in range(3)]
        ahead = ahead + recv[k, 3]
    for c in range(3):
        o_ref[c] = sums[c]
    o_ref[3] = 1.0 - jnp.exp2(ahead)


def body(sizes, fields, palette):
    n_gz = sizes[2]
    _, nz, ny, nx = fields.shape
    gap, entry, pair = (16, 2, 1) if n_gz > 4 else (4, 1, 1)
    dma = pltpu.SemaphoreType.DMA
    return pl.pallas_call(
        functools.partial(kernel, sizes, gap, entry, pair),
        out_shape=jax.ShapeDtypeStruct((4, ny // n_gz, nx), F32),
        in_specs=[
            pl.BlockSpec(memory_space=pl.ANY),
            pl.BlockSpec(memory_space=pl.ANY),
        ],
        out_specs=pl.BlockSpec(memory_space=pltpu.VMEM),
        scratch_shapes=[
            pltpu.SMEM((2, 3), F32),
            pltpu.VMEM((2, 2, nz, ny + 2 * ROWS, LANES), F32),
            pltpu.VMEM((2, 2, ny, nx), F32),
            pltpu.VMEM((2, ny, LANES), F32),
            pltpu.VMEM((2, ny, LANES), F32),
            pltpu.VMEM((2, nz, ny, LANES), F32),
            pltpu.VMEM((2, nz, ny, LANES), F32),
            pltpu.VMEM((n_gz, 6, ROWS, LANES), F32),
            pltpu.VMEM((n_gz, 4, ROWS, nx), F32),
            pltpu.VMEM((n_gz, 4, ROWS, nx), F32),
            dma(()),
            pltpu.SemaphoreType.REGULAR,
            dma((n_gz,)),
            dma((2,)),
            dma((n_gz,)),
            dma((2,)),
            dma((2,)),
            dma(()),
            dma((n_gz,)),
            dma(()),
            dma(()),
        ],
        compiler_params=pltpu.CompilerParams(
            collective_id=0, has_side_effects=True, vmem_limit_bytes=58 << 20
        ),
    )(palette, fields)


def solution(mesh):
    sizes = tuple(mesh.shape[axis] for axis in ("iy", "ix", "gz"))
    return jax.shard_map(
        functools.partial(body, sizes),
        mesh=mesh,
        in_specs=(P(None, "gz", "iy", "ix"), P()),
        out_specs=P(None, ("iy", "gz"), "ix"),
        check_vma=False,
    )
```

time: 35.8 us -> 23.8 us (0.66)
  Pallas kernels: 31 us -> 22.3 us
  local copies, waits for them, and re-layouts: 4.68 us -> 1.38 us
    pallas_call x1, Pallas kernels: 31 us -> 22.3 us  [body(): pl.pallas_call(functools.partial(kernel, sizes, gap, entry, pair), out_sh...]
    unnamed x5 -> x1, local copies, waits for them, and re-layouts: 4.68 us -> 1.38 us
where the time goes in v3:
time: 23.8 us; the launch traced here: 23.7 us
  Pallas kernels  22.3 us (94%)
  local copies, waits for them, and re-layouts  1.38 us (6%)
    pallas_call x1, Pallas kernels, body(): pl.pallas_call(functools.partial(kernel, sizes, gap, entry, pair), out_sh...  22.3 us
    unnamed x1, local copies, waits for them, and re-layouts  1.38 us

profile of v3, /device:TPU:1, one launch (start us, length us, event | category | flops | bytes accessed | tf_op | source)
XLA Modules:
  0.0 23.7 jit_solution(8063548060952465378)
XLA Ops:
  0.0 22.3 %shard_map.28 = f32[4,8,256]{2,1,0:T(8,128)} custom-call(f32[2,3]{1,0:T(2,128)} %p_ref.1, f32[2,32,128,256]{3,2,1,0:T(8,128)} %f_ref.1), custom_call_target="tpu_custom_call" | custom-call | tf_op jit(solution)/shard_map/pallas_call | solution.py:431
  22.3 1.4 %copy.4 = f32[4,8,256]{2,1,0:T(8,128)} copy(f32[4,8,256]{2,1,0:T(8,128)} %shard_map.28) | data formatting | bytes 65536

commit v4 on v3

--- a/solution.py
+++ b/solution.py
@@ -8,13 +8,13 @@
 from jax.sharding import PartitionSpec as P
 
 MESH = pl.DeviceIdType.MESH
+
 F32 = jnp.float32
 LANES = 128
 ROWS = 8
 LOG2E = 1.4426950408889634
 C1 = 0.005 * LOG2E
 C2 = 0.016 * LOG2E
-
 
 def cell(dz, dy, dx, s, ez, ey, ex, u, pal, nz, ny):
     r = lax.rsqrt(dz * dz + dy * dy + dx * dx + 4.0)
@@ -25,9 +25,8 @@
     tints = [jnp.tanh(pal[0][c] * u + pal[1][c]) for c in range(3)]
     return depth, light, tints
 
-
 def kernel(
-    sizes, gap, entry, pair,
+    sizes, gap, entry, pair, cut,
     p_ref, f_ref, o_ref,
     pal_ref, vol, zh, hs, hx, outs, ins, inner, part, recv,
     pal_sem, all_sem, load_sem, zsend, zrecv, ysend, yrecv, xsend, xrecv, asend, arecv,
@@ -36,7 +35,6 @@
     nz, ny = f_ref.shape[1], f_ref.shape[2]
     nb = n_gz
     iy, ix, g = lax.axis_index("iy"), lax.axis_index("ix"), lax.axis_index("gz")
-    sgn = jnp.where(g < nb // 2, 1, -1)
     hh, hc = 1 - ix, ix
     top, bottom = ROWS - 1, ROWS + ny
 
@@ -44,7 +42,7 @@
         return lax.rem(i + 2 * n, n)
 
     def order(i):
-        return wrap(g + sgn * (i + 1), nb)
+        return lax.rem(i + 1, nb)
 
     ring = 4 if nb > 4 else nb
     cols = nb // ring
@@ -56,11 +54,14 @@
 
     turns = sorted(range(nb), key=lambda o: (-hops(o), -min(o % ring, ring - o % ring), o))
 
-    def far_first(j, gx, gy):
-        o = jnp.int32(0)
-        for k, turn in enumerate(turns):
-            o = o + jnp.where(j == k, turn, 0)
-        return wrap(gx + lax.div(o, ring), cols) * ring + wrap(gy + lax.rem(o, ring), ring)
+    def turn(j):
+        o = jnp.int32(turns[-1])
+        for k in range(nb - 1):
+            o = jnp.where(j == k, turns[k], o)
+        return lax.div(o, ring), lax.rem(o, ring)
+
+    def seen_from(col, row, step):
+        return wrap(col + step[0], cols) * ring + wrap(row + step[1], ring)
 
     def rows8(b):
         return pl.ds(pl.multiple_of(ROWS * b, ROWS), ROWS)
@@ -69,10 +70,9 @@
         return pl.ds(pl.multiple_of(ROWS * b, ROWS) + by, ROWS)
 
     def load(l, half):
-        b = wrap(g + sgn * l, nb)
         return pltpu.make_async_copy(
-            f_ref.at[:, :, rows8(b), pl.ds(half * LANES, LANES)],
-            vol.at[half, :, :, shifted(b, ROWS), :],
+            f_ref.at[:, :, rows8(l), pl.ds(half * LANES, LANES)],
+            vol.at[half, :, :, shifted(l, ROWS), :],
             load_sem.at[l],
         )
 
@@ -86,10 +86,6 @@
 
     def wait_load(l):
         landed(vol.at[:, :, :, pl.ds(ROWS, ROWS), :], load_sem.at[l])
-
-    colors = pltpu.make_async_copy(p_ref, pal_ref, pal_sem)
-    colors.start()
-    lax.fori_loop(0, pair + 2, start_load, 0)
 
     barrier = pltpu.get_barrier_semaphore()
 
@@ -123,6 +119,9 @@
     for there in (iy > 0, iy < n_iy - 1, skew_up, skew_down):
         beside = beside + jnp.where(there, 1, 0)
 
+    colors = pltpu.make_async_copy(p_ref, pal_ref, pal_sem)
+    colors.start()
+    lax.fori_loop(0, pair + 2, start_load, 0)
     lax.fori_loop(pair + 2, nb, start_load, 0)
 
     def y_copy(side, half, remote):
@@ -147,24 +146,27 @@
             device_id={"gz": g - 1 if side else g + 1}, device_id_type=MESH,
         )
 
+    up, down = [(lax.div(n, ring), lax.rem(n, ring)) for n in (g + 1, g + nb - 1)]
+
     def z_start(j, _):
+        step = turn(j)
+
         @pl.when(g < nb - 1)
         def _():
-            z_copy(0, far_first(j, lax.div(g + 1, ring), lax.rem(g + 1, ring)), True).start()
+            z_copy(0, seen_from(*up, step), True).start()
 
         @pl.when(g > 0)
         def _():
-            z_copy(1, far_first(j, lax.div(g - 1, ring), lax.rem(g - 1, ring)), True).start()
-
-        @pl.when(g == 0)
-        def _():
-            z_copy(0, j, False).start()
-
-        @pl.when(g == nb - 1)
-        def _():
-            z_copy(1, j, False).start()
+            z_copy(1, seen_from(*down, step), True).start()
 
         return 0
+
+    def z_clamp(side):
+        def one(b, _):
+            z_copy(side, b, False).start()
+            return 0
+
+        lax.fori_loop(0, nb, one, 0)
 
     def y_start():
         for half in range(2):
@@ -280,12 +282,12 @@
                     out = pltpu.roll(h, out_roll, 1)
                     outs[f, z, rows8(b), :] = out
                     edges[k][f].append((h, out))
-                    if 0 < z < nz - 1:
+                    if 0 < z < cut:
                         now.append(at(hc, f, z, b))
                         d, inward = inner_dx(f, z, b, now[f], out)
                         ins[f, z, rows8(b), :] = inward
                         dx.append(d)
-                if 0 < z < nz - 1:
+                if 0 < z < cut:
                     states[k] = add(states[k], *shade(hc, z, b, now, dx))
         for k, b in enumerate(blocks):
             for f in range(2):
@@ -294,33 +296,35 @@
                 inner[b, c] = states[k][c]
 
     def outer_half(blocks):
-        ends = [{} for _ in blocks]
+        fronts = [None for _ in blocks]
+        backs = [clean() for _ in blocks]
         states = [clean() for _ in blocks]
         for z in range(nz):
             for k, b in enumerate(blocks):
                 now = [at(hh, f, z, b) for f in range(2)]
                 out = [outs[f, z, rows8(b), :] for f in range(2)]
-                if 0 < z < nz - 1:
+                if 0 < z < cut:
                     inward = [ins[f, z, rows8(b), :] for f in range(2)]
                 else:
                     mine = [at(hc, f, z, b) for f in range(2)]
                     pairs = [inner_dx(f, z, b, mine[f], out[f]) for f in range(2)]
                     inward = [p[1] for p in pairs]
-                    ends[k][z] = shade(hc, z, b, mine, [p[0] for p in pairs])
+                    shaded = shade(hc, z, b, mine, [p[0] for p in pairs])
+                    if z == 0:
+                        fronts[k] = add(clean(), *shaded)
+                    else:
+                        backs[k] = add(backs[k], *shaded)
                 dx = [outer_dx(f, z, b, now[f], out[f], inward[f]) for f in range(2)]
                 states[k] = add(states[k], *shade(hh, z, b, now, dx))
         for k, b in enumerate(blocks):
             keep(b, hh, states[k])
-            (d0, light0, tints0), (d1, light1, tints1) = ends[k][0], ends[k][nz - 1]
+            front, back = fronts[k], backs[k]
             mid = [inner[b, c] for c in range(6)]
-            t0 = jnp.exp2(d0)
-            lit0 = (1.0 - t0) * light0
-            depth = d0 + mid[0] + d1
-            lit1 = (t0 * mid[1] - jnp.exp2(depth)) * light1
-            sums = [lit0 + t0 * mid[2] + lit1] + [
-                lit0 * tints0[c] + t0 * mid[3 + c] + lit1 * tints1[c] for c in range(3)
-            ]
-            keep(b, hc, [depth, None] + sums)
+            keep(
+                b, hc,
+                [front[0] + mid[0] + back[0], None]
+                + [front[c] + front[1] * (mid[c] + mid[1] * back[c]) for c in range(2, 6)],
+            )
 
     def keep(b, half, state):
         to = pl.ds(pl.multiple_of(half * LANES, LANES), LANES)
@@ -349,6 +353,14 @@
         lax.fori_loop(0, entry, columns, 0)
         lax.fori_loop(0, nb, z_start, 0)
 
+        @pl.when(g == 0)
+        def _():
+            z_clamp(0)
+
+        @pl.when(g == nb - 1)
+        def _():
+            z_clamp(1)
+
     def step(s, _):
         @pl.when(s == entry // pair)
         def _():
@@ -383,7 +395,7 @@
         @pl.when(i >= gap)
         def _():
             j = i - gap
-            blocks = [far_first(j + k, gx, gy) for k in range(pair)]
+            blocks = [seen_from(gx, gy, turn(j + k)) for k in range(pair)]
             for k in range(pair):
                 x_copy(blocks[k]).wait_recv()
                 landed(zh.at[:, :, rows8(blocks[k]), :], zrecv.at[blocks[k]])
@@ -422,14 +434,14 @@
         o_ref[c] = sums[c]
     o_ref[3] = 1.0 - jnp.exp2(ahead)
 
-
 def body(sizes, fields, palette):
     n_gz = sizes[2]
     _, nz, ny, nx = fields.shape
     gap, entry, pair = (16, 2, 1) if n_gz > 4 else (4, 1, 1)
+    cut = nz - 12 if nz > 16 else nz - 3
     dma = pltpu.SemaphoreType.DMA
     return pl.pallas_call(
-        functools.partial(kernel, sizes, gap, entry, pair),
+        functools.partial(kernel, sizes, gap, entry, pair, cut),
         out_shape=jax.ShapeDtypeStruct((4, ny // n_gz, nx), F32),
         in_specs=[
             pl.BlockSpec(memory_space=pl.ANY),
@@ -460,10 +472,9 @@
             dma(()),
         ],
         compiler_params=pltpu.CompilerParams(
-            collective_id=0, has_side_effects=True, vmem_limit_bytes=58 << 20
+            collective_id=0, has_side_effects=True, vmem_limit_bytes=50 << 20
         ),
     )(palette, fields)
-
 
 def solution(mesh):
     sizes = tuple(mesh.shape[axis] for axis in ("iy", "ix", "gz"))

time: 23.8 us -> 22.8 us (0.958)
  Pallas kernels: 22.3 us -> 21.4 us
    pallas_call x1, Pallas kernels: 22.3 us -> 21.4 us  [body(): pl.pallas_call(functools.partial(kernel, sizes, gap, entry, pair, cut), o...]
    unnamed x1 -> x3, local copies, waits for them, and re-layouts: 1.38 us -> 1.3 us
where the time goes in v4:
time: 22.8 us; the launch traced here: 22.7 us
  Pallas kernels  21.4 us (94%)
  local copies, waits for them, and re-layouts  1.3 us (6%)
    pallas_call x1, Pallas kernels, body(): pl.pallas_call(functools.partial(kernel, sizes, gap, entry, pair, cut), o...  21.4 us
    unnamed x3, local copies, waits for them, and re-layouts  1.3 us

profile of v4, /device:TPU:1, one launch (start us, length us, event | category | flops | bytes accessed | tf_op | source)
XLA Modules:
  0.0 22.7 jit_solution(10573545460788463837)
XLA Ops:
  0.0 0.0 copy-start
  0.0 0.7 %copy-done = f32[2,3]{1,0:T(2,128)S(1)} copy-done((f32[2,3]{1,0:T(2,128)S(1)}, f32[2,3]{1,0:T(2,128)}, u32[]{:S(2)}) %copy-start) | copy-done | bytes 48
  0.7 21.4 %shard_map.28 = f32[4,8,256]{2,1,0:T(8,128)S(1)} custom-call(f32[2,3]{1,0:T(2,128)S(1)} %copy-done, f32[2,32,128,256]{3,2,1,0:T(8,128)} %f_ref.1), custom_call_target="tpu_custom_call" | custom-call | tf_op jit(solution)/shard_map/pallas_call | solution.py:443
  22.1 0.6 %copy.4 = f32[4,8,256]{2,1,0:T(8,128)} copy(f32[4,8,256]{2,1,0:T(8,128)S(1)} %shard_map.28) | data formatting | bytes 65536
Async XLA Ops:
  0.0 0.7 %copy-start = (f32[2,3]{1,0:T(2,128)S(1)}, f32[2,3]{1,0:T(2,128)}, u32[]{:S(2)}) copy-start(f32[2,3]{1,0:T(2,128)} %p_ref.1) | copy-start | bytes 76

commit v5 on v4

--- a/solution.py
+++ b/solution.py
@@ -52,7 +52,7 @@
         dx, dy = o // ring, o % ring
         return min(dx, cols - dx) + min(dy, ring - dy)
 
-    turns = sorted(range(nb), key=lambda o: (-hops(o), -min(o % ring, ring - o % ring), o))
+    turns = sorted(range(nb), key=lambda o: (-min(o % ring, ring - o % ring), -min(o // ring, cols - o // ring), o))
 
     def turn(j):
         o = jnp.int32(turns[-1])
@@ -438,7 +438,7 @@
     n_gz = sizes[2]
     _, nz, ny, nx = fields.shape
     gap, entry, pair = (16, 2, 1) if n_gz > 4 else (4, 1, 1)
-    cut = nz - 12 if nz > 16 else nz - 3
+    cut = nz - 16 if nz > 16 else nz - 3
     dma = pltpu.SemaphoreType.DMA
     return pl.pallas_call(
         functools.partial(kernel, sizes, gap, entry, pair, cut),

time: 22.8 us -> 22.2 us (0.974)
  Pallas kernels: 21.4 us -> 20.8 us
    pallas_call x1, Pallas kernels: 21.4 us -> 20.8 us  [body(): pl.pallas_call(functools.partial(kernel, sizes, gap, entry, pair, cut), o...]
where the time goes in v5:
time: 22.2 us; the launch traced here: 22.1 us
  Pallas kernels  20.8 us (94%)
  local copies, waits for them, and re-layouts  1.3 us (6%)
    pallas_call x1, Pallas kernels, body(): pl.pallas_call(functools.partial(kernel, sizes, gap, entry, pair, cut), o...  20.8 us
    unnamed x3, local copies, waits for them, and re-layouts  1.3 us

profile of v5, /device:TPU:1, one launch (start us, length us, event | category | flops | bytes accessed | tf_op | source)
XLA Modules:
  0.0 22.1 jit_solution(2990334712092956354)
XLA Ops:
  0.0 0.0 copy-start
  0.0 0.7 %copy-done = f32[2,3]{1,0:T(2,128)S(1)} copy-done((f32[2,3]{1,0:T(2,128)S(1)}, f32[2,3]{1,0:T(2,128)}, u32[]{:S(2)}) %copy-start) | copy-done | bytes 48
  0.7 20.8 %shard_map.28 = f32[4,8,256]{2,1,0:T(8,128)S(1)} custom-call(f32[2,3]{1,0:T(2,128)S(1)} %copy-done, f32[2,32,128,256]{3,2,1,0:T(8,128)} %f_ref.1), custom_call_target="tpu_custom_call" | custom-call | tf_op jit(solution)/shard_map/pallas_call | solution.py:443
  21.5 0.6 %copy.4 = f32[4,8,256]{2,1,0:T(8,128)} copy(f32[4,8,256]{2,1,0:T(8,128)S(1)} %shard_map.28) | data formatting | bytes 65536
Async XLA Ops:
  0.0 0.7 %copy-start = (f32[2,3]{1,0:T(2,128)S(1)}, f32[2,3]{1,0:T(2,128)}, u32[]{:S(2)}) copy-start(f32[2,3]{1,0:T(2,128)} %p_ref.1) | copy-start | bytes 76

commit v6 on v5

--- a/solution.py
+++ b/solution.py
@@ -406,7 +406,6 @@
         return 0
 
     lax.fori_loop(0, (nb + gap) // pair, step, 0)
-    recv[g] = part[g]
     landed(hs, xsend)
 
     @pl.when(g < nb - 1)
@@ -422,7 +421,7 @@
         def _(side=side):
             landed(vol.at[:, :, :, pl.ds(0, 1), :], ysend.at[side])
 
-    landed(part.at[pl.ds(0, nb - 1)], asend)
+    recv[g] = part[g]
     landed(recv.at[pl.ds(0, nb - 1)], arecv)
     ahead = jnp.zeros(recv.shape[2:], F32)
     sums = [jnp.zeros(recv.shape[2:], F32) for _ in range(3)]
@@ -433,6 +432,7 @@
     for c in range(3):
         o_ref[c] = sums[c]
     o_ref[3] = 1.0 - jnp.exp2(ahead)
+    landed(part.at[pl.ds(0, nb - 1)], asend)
 
 def body(sizes, fields, palette):
     n_gz = sizes[2]

time: 22.2 us -> 22.2 us (level)
  no operation moved by 1% of the time
where the time goes in v6:
time: 22.2 us; the launch traced here: 22.1 us
  Pallas kernels  20.8 us (94%)
  local copies, waits for them, and re-layouts  1.3 us (6%)
    pallas_call x1, Pallas kernels, body(): pl.pallas_call(functools.partial(kernel, sizes, gap, entry, pair, cut), o...  20.8 us
    unnamed x3, local copies, waits for them, and re-layouts  1.3 us

profile of v6, /device:TPU:1, one launch (start us, length us, event | category | flops | bytes accessed | tf_op | source)
XLA Modules:
  0.0 22.1 jit_solution(6803333133438815260)
XLA Ops:
  0.0 0.0 copy-start
  0.0 0.7 %copy-done = f32[2,3]{1,0:T(2,128)S(1)} copy-done((f32[2,3]{1,0:T(2,128)S(1)}, f32[2,3]{1,0:T(2,128)}, u32[]{:S(2)}) %copy-start) | copy-done | bytes 48
  0.7 20.8 %shard_map.28 = f32[4,8,256]{2,1,0:T(8,128)S(1)} custom-call(f32[2,3]{1,0:T(2,128)S(1)} %copy-done, f32[2,32,128,256]{3,2,1,0:T(8,128)} %f_ref.1), custom_call_target="tpu_custom_call" | custom-call | tf_op jit(solution)/shard_map/pallas_call | solution.py:443
  21.5 0.6 %copy.4 = f32[4,8,256]{2,1,0:T(8,128)} copy(f32[4,8,256]{2,1,0:T(8,128)S(1)} %shard_map.28) | data formatting | bytes 65536
Async XLA Ops:
  0.0 0.7 %copy-start = (f32[2,3]{1,0:T(2,128)S(1)}, f32[2,3]{1,0:T(2,128)}, u32[]{:S(2)}) copy-start(f32[2,3]{1,0:T(2,128)} %p_ref.1) | copy-start | bytes 76
